TPU v7x, 32 devices: a whole 2x2x4 slice. The times are simulated.
32 devices in a mesh: mem: 4 (over y, x), lon: 8 (over z, core).
Axes of the slice: x: 2, y: 2, z: 4, core: 2. Of those that a mesh axis runs over, the one named last changes fastest.
Arguments:
- members: float32 [16, 256, 12, 720], P('mem', 'lon'), may hold values from -6 to 6
- control: float32 [256, 12, 720], P('lon', None, 'mem'), may hold values from -6 to 6
- sea_mask: int32 [256, 12], P('lon'), may hold values 0 or 1
- depth_class: int32 [256, 12], P('lon'), may hold values from 0 to 3
- wind_dir: int32 [256, 12], P('lon'), may hold values from 0 to 23
- growth: float32 [30], replicated, may hold values from 0.2 to 2
- kernel: float32 [720, 720], replicated, may hold values from -0.21875 to 0.21875
Outputs:
- spectra: float32 [16, 256, 12, 720], P('mem', 'lon')
All inputs are finite; a program needn't handle non-finite values. No bound on the sum of `sea_mask` on one device may be relied on, other than what follows from the above.
Results may differ from a plain program's by a relative error of at most 0.0001.
Values sent between devices are 32-bit elements; how exact they have to be, the bound alone decides.
A program may use at most 128 MiB of HBM per device.

v0:
```python
import math
import jax
import jax.numpy as jnp
from jax import lax
from jax.sharding import PartitionSpec as P

DIRS = 24
FREQS = 30


def extended(x, sides, width):
    for axis, dim in sides:
        count, length = (lax.axis_size(axis), x.shape[dim])
        up = [(i, (i + 1) % count) for i in range(count)]
        down = [(j, i) for i, j in up]
        last = lax.slice_in_dim(x, length - width, length, axis=dim)
        initial = lax.slice_in_dim(x, 0, width, axis=dim)
        before = lax.ppermute(last, axis, up)
        after = lax.ppermute(initial, axis, down)
        x = jnp.concatenate([before, x, after], axis=dim)
    return x


def wave_tables(sea_mask, depth_class, wind_dir, growth):
    cells_lon, rows_lat = sea_mask.shape
    frequency = 0.04 * jnp.power(jnp.float32(1.1), jnp.arange(FREQS).astype(jnp.float32))
    deep_speed = 9.81 / (4.0 * math.pi * frequency)
    depths = jnp.array([10.0, 30.0, 80.0, 200.0], jnp.float32)
    shallow = jnp.sqrt(9.81 * depths)
    group_speed = jnp.minimum(deep_speed[None, :], shallow[:, None])
    fastest = 9.81 / (4.0 * math.pi * 0.04)
    onehot = (depth_class[..., None] == jnp.arange(4)).astype(jnp.float32)
    cell_speed = 0.7 * jnp.sum(onehot[..., None] * group_speed, axis=2) / fastest
    angles = 2.0 * math.pi * jnp.arange(DIRS).astype(jnp.float32) / DIRS
    zonal_speed = (cell_speed[:, :, None, :] * jnp.cos(angles)[:, None]).reshape(
        cells_lon, rows_lat, DIRS * FREQS
    )
    merid_speed = (cell_speed[:, :, None, :] * jnp.sin(angles)[:, None]).reshape(
        cells_lon, rows_lat, DIRS * FREQS
    )
    relative = (jnp.arange(DIRS)[None, None, :] - wind_dir[..., None]).astype(jnp.float32)
    alignment = jnp.maximum(jnp.cos(2.0 * math.pi * relative / DIRS), 0.0)
    wind_gain = (alignment[..., None] * growth[None, None, None, :]).reshape(
        cells_lon, rows_lat, DIRS * FREQS
    )
    ocean = sea_mask.astype(jnp.float32)[..., None]
    return (zonal_speed, merid_speed, wind_gain, ocean)


def advect(centre, west_side, east_side, zonal_speed, merid_speed):
    lat_pad = jnp.pad(centre, ((0, 0), (0, 0), (1, 1), (0, 0)))
    south_side = lat_pad[:, :, :-2]
    north_side = lat_pad[:, :, 2:]
    flux = jnp.maximum(zonal_speed, 0.0) * (centre - west_side) + jnp.minimum(zonal_speed, 0.0) * (
        east_side - centre
    )
    flux = (
        flux
        + jnp.maximum(merid_speed, 0.0) * (centre - south_side)
        + jnp.minimum(merid_speed, 0.0) * (north_side - centre)
    )
    return centre - flux


def source(field, wind_gain, ocean, kernel):
    energy = jnp.mean(field * field, axis=-1, keepdims=True)
    shape = field.shape
    transfer = jnp.dot(
        field.reshape(-1, shape[-1]),
        kernel,
        precision=lax.Precision.HIGHEST,
        preferred_element_type=jnp.float32,
    ).reshape(shape)
    return (field + 0.1 * (wind_gain * field - 0.5 * energy * field + transfer)) * ocean


def padded_step(padded, tables, kernel):
    zonal_speed, merid_speed, wind_gain, ocean = tables
    moved = advect(padded[:, 1:-1], padded[:, :-2], padded[:, 2:], zonal_speed, merid_speed)
    return source(moved, wind_gain, ocean, kernel)


def thin_step(field, tables, kernel):
    padded = extended(field, (("lon", 1),), 1)
    return padded_step(padded, tables, kernel)


def shards(members, control, sea_mask, depth_class, wind_dir, growth, kernel):
    member_count = members.shape[0] * lax.axis_size("mem")
    local_total = jnp.sum(members, axis=0)
    tables = wave_tables(sea_mask, depth_class, wind_dir, growth)
    ocean = tables[3]
    member_total = lax.psum(local_total, "mem")
    control_full = lax.all_gather(control, "mem", axis=2, tiled=True)
    field = (members - member_total / member_count + control_full) * ocean
    field = thin_step(field, tables, kernel)
    field = thin_step(field, tables, kernel)
    return field


def solution(mesh):
    return jax.shard_map(
        shards,
        mesh=mesh,
        in_specs=(
            P("mem", "lon", None, None),
            P("lon", None, "mem"),
            P("lon", None),
            P("lon", None),
            P("lon", None),
            P(),
            P(),
        ),
        out_specs=P("mem", "lon", None, None),
        check_vma=False,
    )
```

profile of v0, /device:TPU:0, one launch (start us, length us, event | category | flops | bytes accessed | tf_op | source)
XLA Modules:
  0.0 206.2 jit_solution(917678572837277976)
XLA Ops:
  6.5 0.0 copy-start
  6.5 0.0 copy-start.10
  6.5 0.0 copy-start.5
  6.5 0.0 copy-start.7
  6.5 0.0 copy-start.9
  6.5 0.0 copy-start.8
  6.6 0.0 copy-start.6
  6.6 0.0 all-reduce.4.cloned.1.call-start
  6.6 4.0 %reduce_sum.36 = f32[32,12,720]{2,0,1:T(8,128)} reduce(f32[4,32,12,720]{3,1,2,0:T(8,128)} %param.8, f32[]{:T(128)} %constant.14.clone.1), dimensions={0}, to_apply=%region_0.0 | reduce | flops 829440 | bytes 5529604 | tf_op jit(solution)/shard_map/reduce_sum | solution.py:90
  10.6 0.0 all-reduce.4.cloned.1.call-update
  10.7 0.0 all-gather.2.cloned.1.call-start
  10.7 0.0 copy-done.5
  10.7 2.0 copy.14
  12.7 0.0 all-gather.2.cloned.1.call-update
  12.8 0.0 copy-done.7
  12.8 0.1 mul.260
  12.9 0.1 mul.261
  13.0 0.1 mul.252
  13.1 0.1 mul.253
  13.2 0.0 copy-done.9
  13.2 0.1 mul.271
  13.3 0.0 copy-done.10
  13.3 0.1 broadcast_minimum_fusion
  13.4 0.0 copy-done.8
  13.4 0.5 multiply_reduce_fusion.2
  14.0 0.1 copy.16
  14.1 0.0 copy-done.6
  14.1 0.7 cosine_maximum_fusion
  14.8 3.2 %mul.268 = f32[32,12,24,30]{3,2,0,1:T(8,128)} broadcast(f32[32,12,24]{2,0,1:T(8,128)S(1)} %cosine_maximum_fusion), dimensions={0,1,2} | broadcast | bytes 1142784 | tf_op jit(solution)/shard_map/mul | solution.py:43
  18.1 4.9 %mul.269 = f32[32,12,720]{2,0,1:T(8,128)} reshape(f32[32,12,24,30]{3,2,0,1:T(8,128)} %mul.268) | data formatting | bytes 2211840 | tf_op jit(solution)/shard_map/mul | solution.py:43
  22.9 2.5 %mul.250 = f32[32,12,24,30]{3,2,0,1:T(8,128)} broadcast(f32[32,12,30]{2,0,1:T(8,128)S(1)} %copy.16), dimensions={0,1,3} | broadcast | bytes 1152000 | tf_op jit(solution)/shard_map/mul | solution.py:35
  25.4 4.6 %mul.251 = f32[32,12,720]{2,0,1:T(8,128)} reshape(f32[32,12,24,30]{3,2,0,1:T(8,128)} %mul.250) | data formatting | bytes 2211840 | tf_op jit(solution)/shard_map/mul | solution.py:35
  30.0 3.3 %multiply_maximum_fusion.1 = (f32[32,12,720]{2,0,1:T(8,128)S(1)}, f32[32,12,720]{2,0,1:T(8,128)}, f32[32,12,720]{2,0,1:T(8,128)}, f32[32,12,720]{2,0,1:T(8,128)}) fusion(f32[32,12,720]{2,0,1:T(8,128)} %mul.251, f32[720]{0:T(1024)S(1)} %mul.253, f32[720]{0:T(1024)S(1)} %mul.261), kind=kLoop, calls=%fused_computation.44 | loop fusion | flops 1658880 | bytes 5535360 | tf_op jit(solution)/shard_map/max | solution.py:54
  33.3 34.7 %all-reduce.4.cloned.1.call-done = f32[32,12,720]{2,0,1:T(8,128)} async-done(((f32[32,12,720]{2,0,1:T(8,128)}), f32[32,12,720]{2,0,1:T(8,128)}) %all-reduce.4.cloned.1.call-update) | async-done | bytes 1105936 | tf_op jit(solution)/shard_map/psum | solution.py:93
  68.0 2.4 %broadcast_multiply_fusion.1 = f32[32,12,720]{2,0,1:T(8,128)} fusion(f32[32,12,720]{2,0,1:T(8,128)} %all-reduce.4.cloned.1.call-done), kind=kLoop, calls=%fused_computation.47 | loop fusion | flops 276480 | bytes 2211840 | tf_op jit(solution)/shard_map/div | solution.py:95
  70.4 66.5 %all-gather.2.cloned.1.call-done = f32[32,12,720]{0,1,2:T(8,128)} async-done(((f32[32,12,180]{0,1,2:T(8,128)}), f32[32,12,720]{0,1,2:T(8,128)}) %all-gather.2.cloned.1.call-update) | async-done | bytes 1105936 | tf_op jit(solution)/shard_map/all_gather | solution.py:94
  136.9 5.4 %copy.15 = f32[32,12,720]{2,0,1:T(8,128)} copy(f32[32,12,720]{0,1,2:T(8,128)} %all-gather.2.cloned.1.call-done) | data formatting | bytes 2211840 | tf_op jit(solution)/shard_map/all_gather | solution.py:94
  142.3 0.0 copy-start.4
  142.3 0.0 copy-start.1
  142.3 0.0 copy-start.2
  142.3 0.0 copy-start.3
  142.3 4.1 %add_multiply_fusion.2 = f32[4,32,12,720]{3,1,2,0:T(8,128)S(1)} fusion(f32[4,32,12,720]{3,1,2,0:T(8,128)} %param.8, f32[32,12]{0,1:T(8,128)S(1)} %convert_element_type.39, f32[32,12,720]{2,0,1:T(8,128)} %copy.15, f32[32,12,720]{2,0,1:T(8,128)} %broadcast_multiply_fusion.1), kind=kLoop, calls=%fused_computation.36 | loop fusion | flops 3317760 | bytes 11060736 | tf_op jit(solution)/shard_map/mul | solution.py:95
  146.4 0.2 fusion.38
  146.6 0.1 collective-permute-start
  146.6 3.5 %collective-permute-start.1 = (f32[4,1,12,720]{3,1,2,0:T(1,128)S(1)}, f32[4,1,12,720]{3,1,2,0:T(1,128)S(1)}, u32[]{:S(2)}, u32[]{:S(2)}) collective-permute-start(f32[4,1,12,720]{3,1,2,0:T(1,128)S(1)} %get-tuple-element.12), channel_id=1, source_target_pairs={{1,0},{2,1},{3,2},{4,3},{5,4},{6,5},{7,6},{0,7},{9,8},{10,9},{11,1... | collective-permute-start | bytes 414728 | tf_op jit(solution)/shard_map/ppermute | solution.py:19
  150.2 0.0 copy-done.4
  150.2 0.1 broadcast_multiply_fusion
  150.3 2.9 %collective-permute-done = f32[4,1,12,720]{3,1,2,0:T(1,128)S(1)} collective-permute-done((f32[4,1,12,720]{3,1,2,0:T(1,128)S(1)}, f32[4,1,12,720]{3,1,2,0:T(1,128)S(1)}, u32[]{:S(2)}, u32[]{:S(2)}) %collective-permute-start) | collective-permute-done | bytes 138272 | tf_op jit(solution)/shard_map/ppermute | solution.py:18
  153.1 0.0 collective-permute-done.1
  153.1 0.0 copy-done.1
  153.1 0.0 copy-done.2
  153.2 0.0 copy-done.3
  153.2 4.5 %multiply_reduce_fusion.1 = (f32[4,32,12]{1,2,0:T(8,128)S(1)}, f32[4,32,12,720]{3,1,2,0:T(8,128)S(1)}) fusion(f32[4,32,12,720]{3,1,2,0:T(8,128)S(1)} %add_multiply_fusion.2, f32[32,12,720]{2,0,1:T(8,128)S(1)} %copy-done.2, f32[32,12,720]{2,0,1:T(8,128)S(1)} %copy-done.3, f32[4,1,12,720]{3,1,2,0:T(1,128)S(1)} %collective-permute-done.1, ...), kind=kLoop, calls=%fused_computation.35 | loop fusion | flops 17693184 | bytes 13553664 | tf_op jit(solution)/shard_map/reduce_sum | solution.py:66
  157.7 0.0 copy-done
  157.7 14.8 %add_multiply_fusion.1 = f32[4,32,12,720]{3,1,2,0:T(8,128)S(1)} fusion(f32[4,32,12,720]{3,1,2,0:T(8,128)S(1)} %get-tuple-element.8, f32[4,32,12]{1,2,0:T(8,128)S(1)} %broadcast_multiply_fusion.4, f32[32,12,720]{2,0,1:T(8,128)S(1)} %broadcast_multiply_fusion, f32[32,12]{0,1:T(8,128)S(1)} %convert_element_type.39, f32[720,720]{1,0:T(8,128)S(1)} %copy-done), kind=kOutput, calls=%fused_computation.34 | convolution fusion | flops 9562890240 | bytes 12034560 | tf_op jit(solution)/shard_map/dot_general | solution.py:68
  172.5 0.2 fusion.37
  172.7 1.3 collective-permute-start.2
  174.0 2.3 %collective-permute-start.3 = (f32[4,1,12,720]{3,1,2,0:T(1,128)S(1)}, f32[4,1,12,720]{3,1,2,0:T(1,128)S(1)}, u32[]{:S(2)}, u32[]{:S(2)}) collective-permute-start(f32[4,1,12,720]{3,1,2,0:T(1,128)S(1)} %get-tuple-element.10), channel_id=1, source_target_pairs={{1,0},{2,1},{3,2},{4,3},{5,4},{6,5},{7,6},{0,7},{9,8},{10,9},{11,1... | collective-permute-start | bytes 414728 | tf_op jit(solution)/shard_map/ppermute | solution.py:19
  176.3 4.0 %collective-permute-done.2 = f32[4,1,12,720]{3,1,2,0:T(1,128)S(1)} collective-permute-done((f32[4,1,12,720]{3,1,2,0:T(1,128)S(1)}, f32[4,1,12,720]{3,1,2,0:T(1,128)S(1)}, u32[]{:S(2)}, u32[]{:S(2)}) %collective-permute-start.2) | collective-permute-done | bytes 138272 | tf_op jit(solution)/shard_map/ppermute | solution.py:18
  180.3 0.0 collective-permute-done.3
  180.3 4.3 %multiply_reduce_fusion = (f32[4,32,12]{1,2,0:T(8,128)S(1)}, f32[4,32,12,720]{3,1,2,0:T(8,128)S(1)}) fusion(f32[4,32,12,720]{3,1,2,0:T(8,128)S(1)} %add_multiply_fusion.1, f32[32,12,720]{2,0,1:T(8,128)S(1)} %copy-done.2, f32[32,12,720]{2,0,1:T(8,128)S(1)} %copy-done.3, f32[4,1,12,720]{3,1,2,0:T(1,128)S(1)} %collective-permute-done.3, ...), kind=kLoop, calls=%fused_computation.33 | loop fusion | flops 17693184 | bytes 13553664 | tf_op jit(solution)/shard_map/reduce_sum | solution.py:66
  184.6 14.8 %add_multiply_fusion = f32[4,32,12,720]{3,1,2,0:T(8,128)} fusion(f32[4,32,12,720]{3,1,2,0:T(8,128)S(1)} %get-tuple-element.6, f32[4,32,12]{1,2,0:T(8,128)S(1)} %broadcast_multiply_fusion.3, f32[32,12,720]{2,0,1:T(8,128)S(1)} %broadcast_multiply_fusion, f32[32,12]{0,1:T(8,128)S(1)} %convert_element_type.39, f32[720,720]{1,0:T(8,128)S(1)} %copy-done), kind=kOutput, calls=%fused_computation.32 | convolution fusion | flops 9562890240 | bytes 12034560 | tf_op jit(solution)/shard_map/dot_general | solution.py:68
  (9 shorter events, 0.1 us)
Async XLA Ops:
  6.5 151.1 %copy-start = (f32[720,720]{1,0:T(8,128)S(1)}, f32[720,720]{1,0:T(8,128)}, u32[]{:S(2)}) copy-start(f32[720,720]{1,0:T(8,128)} %param.14) | copy-start | bytes 6220804
  6.5 6.7 %copy-start.10 = (f32[4]{0:T(128)S(1)}, f32[4]{0:T(128)}, u32[]{:S(2)}) copy-start(f32[4]{0:T(128)} %constant.49) | copy-start | bytes 52
  6.5 4.2 %copy-start.5 = (f32[32,12,180]{2,0,1:T(8,128)S(1)}, f32[32,12,180]{2,0,1:T(8,128)}, u32[]{:S(2)}) copy-start(f32[32,12,180]{2,0,1:T(8,128)} %param.9) | copy-start | bytes 829444
  6.5 6.3 %copy-start.7 = (s32[32,12]{0,1:T(8,128)S(1)}, s32[32,12]{0,1:T(8,128)}, u32[]{:S(2)}) copy-start(s32[32,12]{0,1:T(8,128)} %param.10) | copy-start | bytes 4612
  6.5 6.6 %copy-start.9 = (f32[30]{0:T(128)S(1)}, f32[30]{0:T(128)}, u32[]{:S(2)}) copy-start(f32[30]{0:T(128)} %param.13) | copy-start | bytes 364
  6.5 6.8 %copy-start.8 = (s32[32,12]{0,1:T(8,128)S(1)}, s32[32,12]{0,1:T(8,128)}, u32[]{:S(2)}) copy-start(s32[32,12]{0,1:T(8,128)} %param.11) | copy-start | bytes 4612
  6.6 7.6 %copy-start.6 = (s32[32,12]{0,1:T(8,128)S(1)}, s32[32,12]{0,1:T(8,128)}, u32[]{:S(2)}) copy-start(s32[32,12]{0,1:T(8,128)} %param.12) | copy-start | bytes 4612
  6.6 61.4 %all-reduce.4.cloned.1.call-start = ((), (), s32[]{:S(2)}) async-start(), calls=%async_computation | async-start | bytes 2359296 | tf_op jit(solution)/shard_map/psum | solution.py:93
  10.7 126.2 %all-gather.2.cloned.1.call-start = ((), (), s32[]{:S(2)}) async-start(), calls=%async_computation.1 | async-start | bytes 7372800 | tf_op jit(solution)/shard_map/all_gather | solution.py:94
  142.3 7.9 %copy-start.4 = (f32[32,12,720]{2,0,1:T(8,128)S(1)}, f32[32,12,720]{2,0,1:T(8,128)}, u32[]{:S(2)}) copy-start(f32[32,12,720]{2,0,1:T(8,128)} %mul.269) | copy-start | bytes 3317764
  142.3 10.9 %copy-start.1 = (f32[32,12,720]{2,0,1:T(8,128)S(1)}, f32[32,12,720]{2,0,1:T(8,128)}, u32[]{:S(2)}) copy-start(f32[32,12,720]{2,0,1:T(8,128)} %get-tuple-element.14) | copy-start | bytes 3317764
  142.3 10.9 %copy-start.2 = (f32[32,12,720]{2,0,1:T(8,128)S(1)}, f32[32,12,720]{2,0,1:T(8,128)}, u32[]{:S(2)}) copy-start(f32[32,12,720]{2,0,1:T(8,128)} %get-tuple-element.17) | copy-start | bytes 3317764
  142.3 10.9 %copy-start.3 = (f32[32,12,720]{2,0,1:T(8,128)S(1)}, f32[32,12,720]{2,0,1:T(8,128)}, u32[]{:S(2)}) copy-start(f32[32,12,720]{2,0,1:T(8,128)} %get-tuple-element.18) | copy-start | bytes 3317764
  146.6 6.6 %collective-permute-start = (f32[4,1,12,720]{3,1,2,0:T(1,128)S(1)}, f32[4,1,12,720]{3,1,2,0:T(1,128)S(1)}, u32[]{:S(2)}, u32[]{:S(2)}) collective-permute-start(f32[4,1,12,720]{3,1,2,0:T(1,128)S(1)} %get-tuple-element.11), channel_id=1, source_target_pairs={{0,1},{1,2},{2,3},{3,4},{4,5},{5,6},{6,7},{7,0},{8,9},{9,10},{10,1... | collective-permute-start | bytes 414728 | tf_op jit(solution)/shard_map/ppermute | solution.py:18
  146.6 6.5 %collective-permute-start.1 = (f32[4,1,12,720]{3,1,2,0:T(1,128)S(1)}, f32[4,1,12,720]{3,1,2,0:T(1,128)S(1)}, u32[]{:S(2)}, u32[]{:S(2)}) collective-permute-start(f32[4,1,12,720]{3,1,2,0:T(1,128)S(1)} %get-tuple-element.12), channel_id=1, source_target_pairs={{1,0},{2,1},{3,2},{4,3},{5,4},{6,5},{7,6},{0,7},{9,8},{10,9},{11,1... | collective-permute-start | bytes 414728 | tf_op jit(solution)/shard_map/ppermute | solution.py:19
  172.7 7.5 %collective-permute-start.2 = (f32[4,1,12,720]{3,1,2,0:T(1,128)S(1)}, f32[4,1,12,720]{3,1,2,0:T(1,128)S(1)}, u32[]{:S(2)}, u32[]{:S(2)}) collective-permute-start(f32[4,1,12,720]{3,1,2,0:T(1,128)S(1)} %get-tuple-element.9), channel_id=1, source_target_pairs={{0,1},{1,2},{2,3},{3,4},{4,5},{5,6},{6,7},{7,0},{8,9},{9,10},{10,1... | collective-permute-start | bytes 414728 | tf_op jit(solution)/shard_map/ppermute | solution.py:18
  174.0 6.3 %collective-permute-start.3 = (f32[4,1,12,720]{3,1,2,0:T(1,128)S(1)}, f32[4,1,12,720]{3,1,2,0:T(1,128)S(1)}, u32[]{:S(2)}, u32[]{:S(2)}) collective-permute-start(f32[4,1,12,720]{3,1,2,0:T(1,128)S(1)} %get-tuple-element.10), channel_id=1, source_target_pairs={{1,0},{2,1},{3,2},{4,3},{5,4},{6,5},{7,6},{0,7},{9,8},{10,9},{11,1... | collective-permute-start | bytes 414728 | tf_op jit(solution)/shard_map/ppermute | solution.py:19
Sparse Core Ops, SparseCore 0:
  10.8 57.1 all-reduce.3
  70.0 66.8 all-gather.1
where the time goes:
time: 207 us; the launch traced here: 206 us
  waiting for transfers between devices  108 us (52%)
  matrix products  29.6 us (14%)
  other arithmetic  24.1 us (12%)
  local copies, waits for them, and re-layouts  23.5 us (11%)
  between operations  13.7 us (7%)
  starting transfers between devices  7.26 us (4%)
    all_gather x1, waiting for transfers between devices, shards(): control_full = lax.all_gather(control, 'mem', axis=2, tiled=True)  66.5 us
    psum x1, waiting for transfers between devices, shards(): member_total = lax.psum(local_total, 'mem')  34.7 us
    dot_general x2, matrix products, source(): jnp.dot(field.reshape(-1, shape[-1]), kernel, precision=lax.Precision.HIG...  29.6 us
    reduce_sum x2, other arithmetic, source(): energy = jnp.mean(field * field, axis=-1, keepdims=True)  8.77 us
    mul x4, local copies, waits for them, and re-layouts, wave_tables(): alignment[..., None] * growth[None, None, None, :]  8.19 us
    mul x4, local copies, waits for them, and re-layouts, wave_tables(): cell_speed[:, :, None, :] * jnp.cos(angles)[:, None]  7.2 us
    ppermute x2, waiting for transfers between devices, extended(): before = lax.ppermute(last, axis, up)  6.83 us
    ppermute x2, starting transfers between devices, extended(): after = lax.ppermute(initial, axis, down)  5.86 us
  transfers between devices with their start and end apart: 6, of which 4 were waited for; matrix products, arithmetic and copies ran while one was open for 12% of the time, Pallas kernels for 0%

commit v1 on v0

--- a/solution.py
+++ b/solution.py
@@ -3,6 +3,7 @@
 import jax.numpy as jnp
 from jax import lax
 from jax.sharding import PartitionSpec as P
+from jax.lax import axis_index, ppermute, psum
 
 DIRS = 24
 FREQS = 30
@@ -91,7 +92,21 @@
     tables = wave_tables(sea_mask, depth_class, wind_dir, growth)
     ocean = tables[3]
     member_total = lax.psum(local_total, "mem")
-    control_full = lax.all_gather(control, "mem", axis=2, tiled=True)
+    num = psum(1, axis_name="mem")
+    pieces_in = []
+    for rr in range(num):
+        pieces_in.append((rr, (rr + 1) % num))
+    buffers = []
+    for rr in range(num):
+        buffers.append((rr, (rr - 1) % num))
+    state_now, part_next = ([control], [control])
+    for _ in range(num // 2):
+        p_next = ppermute(state_now[-1], axis_name="mem", perm=pieces_in)
+        state_now.append(p_next)
+    for _ in range((num - 1) // 2):
+        part_next.append(ppermute(part_next[-1], axis_name="mem", perm=buffers))
+    q_next = jnp.concatenate([*state_now[::-1], *part_next[1:]], axis=2)
+    control_full = jnp.roll(q_next, (axis_index("mem") - num // 2) * control.shape[2], axis=2)
     field = (members - member_total / member_count + control_full) * ocean
     field = thin_step(field, tables, kernel)
     field = thin_step(field, tables, kernel)

time: 207 us -> 141 us (0.68)
  waiting for transfers between devices: 108 us -> 39.2 us
  starting transfers between devices: 7.26 us -> 12 us
    all_gather x1 -> x0, waiting for transfers between devices: 66.5 us -> none  [shards(): control_full = lax.all_gather(control, 'mem', axis=2, tiled=True)]
    psum x1, waiting for transfers between devices: 34.7 us -> 24.9 us  [shards(): member_total = lax.psum(local_total, 'mem')]
    ppermute x0 -> x3, waiting for transfers between devices: none -> 7.41 us  [the longest x2 7.41 us: shards(): p_next = ppermute(state_now[-1], axis_name='mem', perm=pieces_in)]
    all_gather x1 -> x0, local copies, waits for them, and re-layouts: 5.41 us -> none  [shards(): control_full = lax.all_gather(control, 'mem', axis=2, tiled=True)]
    concatenate x0 -> x1, local copies, waits for them, and re-layouts: none -> 4.86 us  [shards(): jnp.roll(q_next, (axis_index('mem') - num // 2) * control.shape[2], axis=2)]
    ppermute x0 -> x3, starting transfers between devices: none -> 4.77 us  [the longest x2 3.74 us: shards(): p_next = ppermute(state_now[-1], axis_name='mem', perm=pieces_in)]
    dynamic_slice x0 -> x1, local copies, waits for them, and re-layouts: none -> 2.76 us  [shards(): jnp.roll(q_next, (axis_index('mem') - num // 2) * control.shape[2], axis=2)]
  transfers between devices with their start and end apart: 6 -> 8, of which waited for: 4 -> 4; matrix products, arithmetic and copies ran while one was open for 12% -> 23% of each run, Pallas kernels for 0% -> 0%
where the time goes in v1:
time: 141 us
  waiting for transfers between devices  39.2 us (28%)
  matrix products  29.6 us (21%)
  local copies, waits for them, and re-layouts  23.8 us (17%)
  other arithmetic  22.7 us (16%)
  between operations  13.7 us (10%)
  starting transfers between devices  12 us (9%)
    dot_general x2, matrix products, source(): jnp.dot(field.reshape(-1, shape[-1]), kernel, precision=lax.Precision.HIG...  29.6 us
    psum x1, waiting for transfers between devices, shards(): member_total = lax.psum(local_total, 'mem')  24.9 us
    reduce_sum x2, other arithmetic, source(): energy = jnp.mean(field * field, axis=-1, keepdims=True)  8.77 us
    mul x4, local copies, waits for them, and re-layouts, wave_tables(): alignment[..., None] * growth[None, None, None, :]  8.2 us
    ppermute x2, waiting for transfers between devices, shards(): p_next = ppermute(state_now[-1], axis_name='mem', perm=pieces_in)  7.41 us
    mul x4, local copies, waits for them, and re-layouts, wave_tables(): cell_speed[:, :, None, :] * jnp.cos(angles)[:, None]  7.21 us
    ppermute x2, waiting for transfers between devices, extended(): before = lax.ppermute(last, axis, up)  6.84 us
    ppermute x2, starting transfers between devices, extended(): after = lax.ppermute(initial, axis, down)  5.86 us
  transfers between devices with their start and end apart: 8, of which 4 were waited for; matrix products, arithmetic and copies ran while one was open for 23% of the time, Pallas kernels for 0%

profile of v1, /device:TPU:0, one launch (start us, length us, event | category | flops | bytes accessed | tf_op | source)
XLA Modules:
  0.0 141.0 jit_solution(14529423897194188133)
XLA Ops:
  6.5 0.0 copy-start
  6.5 0.0 copy-start.9
  6.5 0.0 copy-start.7
  6.5 0.0 copy-start.6
  6.5 0.0 copy-start.8
  6.5 0.0 copy-start.5
  6.6 0.0 all-reduce.4.cloned.1.call-start
  6.6 3.0 %collective-permute-start = (f32[32,12,180]{2,0,1:T(8,128)}, f32[32,12,180]{2,0,1:T(8,128)}, u32[]{:S(2)}, u32[]{:S(2)}) collective-permute-start(f32[32,12,180]{2,0,1:T(8,128)} %param.9), channel_id=1, source_target_pairs={{0,8},{8,16},{16,24},{24,0},{1,9},{9,17},{17,25},{25,1},{2,10},{10... | collective-permute-start | bytes 829448 | tf_op jit(solution)/shard_map/ppermute | solution.py:104
  9.6 1.0 collective-permute-start.2
  10.6 3.9 %reduce_sum.36 = f32[32,12,720]{2,0,1:T(8,128)} reduce(f32[4,32,12,720]{3,1,2,0:T(8,128)} %param.8, f32[]{:T(128)} %constant.28.clone.1), dimensions={0}, to_apply=%region_0.0 | reduce | flops 829440 | bytes 5529604 | tf_op jit(solution)/shard_map/reduce_sum | solution.py:91
  14.5 0.0 all-reduce.4.cloned.1.call-update
  14.5 0.0 copy-done.7
  14.5 0.0 copy-done.9
  14.6 0.1 broadcast_minimum_fusion
  14.6 0.6 multiply_reduce_fusion.2
  15.3 0.0 copy-done.6
  15.3 0.1 mul.264
  15.4 0.1 mul.265
  15.5 0.1 mul.256
  15.6 0.1 mul.257
  15.7 0.0 copy-done.8
  15.7 0.1 mul.275
  15.8 0.1 copy.11
  15.9 0.0 copy-done.5
  15.9 0.7 cosine_maximum_fusion
  16.7 3.2 %mul.272 = f32[32,12,24,30]{3,2,0,1:T(8,128)} broadcast(f32[32,12,24]{2,0,1:T(8,128)S(1)} %cosine_maximum_fusion), dimensions={0,1,2} | broadcast | bytes 1142784 | tf_op jit(solution)/shard_map/mul | solution.py:44
  19.9 4.9 %mul.273 = f32[32,12,720]{2,0,1:T(8,128)} reshape(f32[32,12,24,30]{3,2,0,1:T(8,128)} %mul.272) | data formatting | bytes 2211840 | tf_op jit(solution)/shard_map/mul | solution.py:44
  24.8 2.5 %mul.254 = f32[32,12,24,30]{3,2,0,1:T(8,128)} broadcast(f32[32,12,30]{2,0,1:T(8,128)S(1)} %copy.11), dimensions={0,1,3} | broadcast | bytes 1152000 | tf_op jit(solution)/shard_map/mul | solution.py:36
  27.3 4.6 %mul.255 = f32[32,12,720]{2,0,1:T(8,128)} reshape(f32[32,12,24,30]{3,2,0,1:T(8,128)} %mul.254) | data formatting | bytes 2211840 | tf_op jit(solution)/shard_map/mul | solution.py:36
  31.8 0.0 collective-permute-done
  31.8 0.8 collective-permute-start.1
  32.6 3.4 %multiply_maximum_fusion.1 = (f32[32,12,720]{2,0,1:T(8,128)S(1)}, f32[32,12,720]{2,0,1:T(8,128)}, f32[32,12,720]{2,0,1:T(8,128)}, f32[32,12,720]{2,0,1:T(8,128)}) fusion(f32[32,12,720]{2,0,1:T(8,128)} %mul.255, f32[720]{0:T(1024)S(1)} %mul.257, f32[720]{0:T(1024)S(1)} %mul.265), kind=kLoop, calls=%fused_computation.44 | loop fusion | flops 1658880 | bytes 5535360 | tf_op jit(solution)/shard_map/max | solution.py:55
  36.0 0.0 collective-permute-done.2
  36.0 7.4 %collective-permute-done.1 = f32[32,12,180]{2,0,1:T(8,128)} collective-permute-done((f32[32,12,180]{2,0,1:T(8,128)}, f32[32,12,180]{2,0,1:T(8,128)}, u32[]{:S(2)}, u32[]{:S(2)}) %collective-permute-start.1) | collective-permute-done | bytes 276512 | tf_op jit(solution)/shard_map/ppermute | solution.py:104
  43.4 4.9 %concatenate.20 = f32[32,12,1440]{2,0,1:T(8,128)} concatenate(f32[32,12,180]{2,0,1:T(8,128)} %collective-permute-done.1, f32[32,12,180]{2,0,1:T(8,128)} %collective-permute-done, f32[32,12,180]{2,0,1:T(8,128)} %param.9, f32[32,12,180]{2,0,1:T(8,128)} %collective-permute-done.2, f32[32,12,180]{2,0,1:T(8,128)} %collective-permute-done.1, f32[32,12,180]{2,0,1:T(8,128)} %collective-permute-done, ...), dimensions={2} | concatenate | bytes 4423680 | tf_op jit(solution)/shard_map/jit(_roll_dynamic)/concatenate | solution.py:109
  48.3 2.8 %constant_dynamic-slice_fusion = f32[32,12,720]{2,0,1:T(8,128)} fusion(f32[32,12,1440]{2,0,1:T(8,128)} %concatenate.20, s32[]{:T(128)S(6)} %select_n.14), kind=kLoop, calls=%fused_computation.59 | loop fusion | bytes 2211844 | tf_op jit(solution)/shard_map/jit(_roll_dynamic)/dynamic_slice | solution.py:109
  51.0 24.9 %all-reduce.4.cloned.1.call-done = f32[32,12,720]{2,0,1:T(8,128)} async-done(((f32[32,12,720]{2,0,1:T(8,128)}), f32[32,12,720]{2,0,1:T(8,128)}) %all-reduce.4.cloned.1.call-update) | async-done | bytes 1105936 | tf_op jit(solution)/shard_map/psum | solution.py:94
  75.9 1.4 broadcast_multiply_fusion.1
  77.3 0.0 copy-start.4
  77.3 0.0 copy-start.1
  77.3 0.0 copy-start.2
  77.3 0.0 copy-start.3
  77.3 3.8 %add_multiply_fusion.2 = f32[4,32,12,720]{3,1,2,0:T(8,128)S(1)} fusion(f32[4,32,12,720]{3,1,2,0:T(8,128)} %param.8, f32[32,12]{0,1:T(8,128)S(1)} %convert_element_type.39, f32[32,12,720]{2,0,1:T(8,128)} %constant_dynamic-slice_fusion, f32[32,12,720]{2,0,1:T(8,128)S(1)} %broadcast_multiply_fusion.1), kind=kLoop, calls=%fused_computation.36 | loop fusion | flops 3317760 | bytes 11060736 | tf_op jit(solution)/shard_map/mul | solution.py:110
  81.1 0.2 fusion.38
  81.3 0.1 collective-permute-start.3
  81.4 3.5 %collective-permute-start.4 = (f32[4,1,12,720]{3,1,2,0:T(1,128)S(1)}, f32[4,1,12,720]{3,1,2,0:T(1,128)S(1)}, u32[]{:S(2)}, u32[]{:S(2)}) collective-permute-start(f32[4,1,12,720]{3,1,2,0:T(1,128)S(1)} %get-tuple-element.12), channel_id=1, source_target_pairs={{1,0},{2,1},{3,2},{4,3},{5,4},{6,5},{7,6},{0,7},{9,8},{10,9},{11,1... | collective-permute-start | bytes 414728 | tf_op jit(solution)/shard_map/ppermute | solution.py:20
  84.9 0.0 copy-done.4
  84.9 0.1 broadcast_multiply_fusion
  85.0 2.9 %collective-permute-done.3 = f32[4,1,12,720]{3,1,2,0:T(1,128)S(1)} collective-permute-done((f32[4,1,12,720]{3,1,2,0:T(1,128)S(1)}, f32[4,1,12,720]{3,1,2,0:T(1,128)S(1)}, u32[]{:S(2)}, u32[]{:S(2)}) %collective-permute-start.3) | collective-permute-done | bytes 138272 | tf_op jit(solution)/shard_map/ppermute | solution.py:19
  87.9 0.0 collective-permute-done.4
  87.9 0.0 copy-done.1
  87.9 0.0 copy-done.2
  87.9 0.0 copy-done.3
  87.9 4.5 %multiply_reduce_fusion.1 = (f32[4,32,12]{1,2,0:T(8,128)S(1)}, f32[4,32,12,720]{3,1,2,0:T(8,128)S(1)}) fusion(f32[4,32,12,720]{3,1,2,0:T(8,128)S(1)} %add_multiply_fusion.2, f32[32,12,720]{2,0,1:T(8,128)S(1)} %copy-done.2, f32[32,12,720]{2,0,1:T(8,128)S(1)} %copy-done.3, f32[4,1,12,720]{3,1,2,0:T(1,128)S(1)} %collective-permute-done.4, ...), kind=kLoop, calls=%fused_computation.35 | loop fusion | flops 17693184 | bytes 13553664 | tf_op jit(solution)/shard_map/reduce_sum | solution.py:67
  92.4 0.0 copy-done
  92.4 14.8 %add_multiply_fusion.1 = f32[4,32,12,720]{3,1,2,0:T(8,128)S(1)} fusion(f32[4,32,12,720]{3,1,2,0:T(8,128)S(1)} %get-tuple-element.8, f32[4,32,12]{1,2,0:T(8,128)S(1)} %broadcast_multiply_fusion.4, f32[32,12,720]{2,0,1:T(8,128)S(1)} %broadcast_multiply_fusion, f32[32,12]{0,1:T(8,128)S(1)} %convert_element_type.39, f32[720,720]{1,0:T(8,128)S(1)} %copy-done), kind=kOutput, calls=%fused_computation.34 | convolution fusion | flops 9562890240 | bytes 12034560 | tf_op jit(solution)/shard_map/dot_general | solution.py:69
  107.3 0.2 fusion.37
  107.5 1.3 collective-permute-start.5
  108.7 2.3 %collective-permute-start.6 = (f32[4,1,12,720]{3,1,2,0:T(1,128)S(1)}, f32[4,1,12,720]{3,1,2,0:T(1,128)S(1)}, u32[]{:S(2)}, u32[]{:S(2)}) collective-permute-start(f32[4,1,12,720]{3,1,2,0:T(1,128)S(1)} %get-tuple-element.10), channel_id=1, source_target_pairs={{1,0},{2,1},{3,2},{4,3},{5,4},{6,5},{7,6},{0,7},{9,8},{10,9},{11,1... | collective-permute-start | bytes 414728 | tf_op jit(solution)/shard_map/ppermute | solution.py:20
  111.1 4.0 %collective-permute-done.5 = f32[4,1,12,720]{3,1,2,0:T(1,128)S(1)} collective-permute-done((f32[4,1,12,720]{3,1,2,0:T(1,128)S(1)}, f32[4,1,12,720]{3,1,2,0:T(1,128)S(1)}, u32[]{:S(2)}, u32[]{:S(2)}) %collective-permute-start.5) | collective-permute-done | bytes 138272 | tf_op jit(solution)/shard_map/ppermute | solution.py:19
  115.0 0.0 collective-permute-done.6
  115.0 4.3 %multiply_reduce_fusion = (f32[4,32,12]{1,2,0:T(8,128)S(1)}, f32[4,32,12,720]{3,1,2,0:T(8,128)S(1)}) fusion(f32[4,32,12,720]{3,1,2,0:T(8,128)S(1)} %add_multiply_fusion.1, f32[32,12,720]{2,0,1:T(8,128)S(1)} %copy-done.2, f32[32,12,720]{2,0,1:T(8,128)S(1)} %copy-done.3, f32[4,1,12,720]{3,1,2,0:T(1,128)S(1)} %collective-permute-done.6, ...), kind=kLoop, calls=%fused_computation.33 | loop fusion | flops 17693184 | bytes 13553664 | tf_op jit(solution)/shard_map/reduce_sum | solution.py:67
  119.3 14.8 %add_multiply_fusion = f32[4,32,12,720]{3,1,2,0:T(8,128)} fusion(f32[4,32,12,720]{3,1,2,0:T(8,128)S(1)} %get-tuple-element.6, f32[4,32,12]{1,2,0:T(8,128)S(1)} %broadcast_multiply_fusion.3, f32[32,12,720]{2,0,1:T(8,128)S(1)} %broadcast_multiply_fusion, f32[32,12]{0,1:T(8,128)S(1)} %convert_element_type.39, f32[720,720]{1,0:T(8,128)S(1)} %copy-done), kind=kOutput, calls=%fused_computation.32 | convolution fusion | flops 9562890240 | bytes 12034560 | tf_op jit(solution)/shard_map/dot_general | solution.py:69
  (9 shorter events, 0.1 us)
Async XLA Ops:
  6.5 85.9 %copy-start = (f32[720,720]{1,0:T(8,128)S(1)}, f32[720,720]{1,0:T(8,128)}, u32[]{:S(2)}) copy-start(f32[720,720]{1,0:T(8,128)} %param.14) | copy-start | bytes 6220804
  6.5 8.0 %copy-start.9 = (f32[4]{0:T(128)S(1)}, f32[4]{0:T(128)}, u32[]{:S(2)}) copy-start(f32[4]{0:T(128)} %constant.78) | copy-start | bytes 52
  6.5 8.0 %copy-start.7 = (s32[32,12]{0,1:T(8,128)S(1)}, s32[32,12]{0,1:T(8,128)}, u32[]{:S(2)}) copy-start(s32[32,12]{0,1:T(8,128)} %param.11) | copy-start | bytes 4612
  6.5 8.8 %copy-start.6 = (s32[32,12]{0,1:T(8,128)S(1)}, s32[32,12]{0,1:T(8,128)}, u32[]{:S(2)}) copy-start(s32[32,12]{0,1:T(8,128)} %param.10) | copy-start | bytes 4612
  6.5 9.1 %copy-start.8 = (f32[30]{0:T(128)S(1)}, f32[30]{0:T(128)}, u32[]{:S(2)}) copy-start(f32[30]{0:T(128)} %param.13) | copy-start | bytes 364
  6.5 9.4 %copy-start.5 = (s32[32,12]{0,1:T(8,128)S(1)}, s32[32,12]{0,1:T(8,128)}, u32[]{:S(2)}) copy-start(s32[32,12]{0,1:T(8,128)} %param.12) | copy-start | bytes 4612
  6.6 69.4 %all-reduce.4.cloned.1.call-start = ((), (), s32[]{:S(2)}) async-start(), calls=%async_computation | async-start | bytes 2359296 | tf_op jit(solution)/shard_map/psum | solution.py:94
  6.6 25.2 %collective-permute-start = (f32[32,12,180]{2,0,1:T(8,128)}, f32[32,12,180]{2,0,1:T(8,128)}, u32[]{:S(2)}, u32[]{:S(2)}) collective-permute-start(f32[32,12,180]{2,0,1:T(8,128)} %param.9), channel_id=1, source_target_pairs={{0,8},{8,16},{16,24},{24,0},{1,9},{9,17},{17,25},{25,1},{2,10},{10... | collective-permute-start | bytes 829448 | tf_op jit(solution)/shard_map/ppermute | solution.py:104
  9.6 26.4 %collective-permute-start.2 = (f32[32,12,180]{2,0,1:T(8,128)}, f32[32,12,180]{2,0,1:T(8,128)}, u32[]{:S(2)}, u32[]{:S(2)}) collective-permute-start(f32[32,12,180]{2,0,1:T(8,128)} %param.9), channel_id=1, source_target_pairs={{0,24},{8,0},{16,8},{24,16},{1,25},{9,1},{17,9},{25,17},{2,26},{10... | collective-permute-start | bytes 829448 | tf_op jit(solution)/shard_map/ppermute | solution.py:107
  31.8 11.6 %collective-permute-start.1 = (f32[32,12,180]{2,0,1:T(8,128)}, f32[32,12,180]{2,0,1:T(8,128)}, u32[]{:S(2)}, u32[]{:S(2)}) collective-permute-start(f32[32,12,180]{2,0,1:T(8,128)} %collective-permute-done), channel_id=1, source_target_pairs={{0,8},{8,16},{16,24},{24,0},{1,9},{9,17},{17,25},{25,1},{2,10},{10... | collective-permute-start | bytes 829448 | tf_op jit(solution)/shard_map/ppermute | solution.py:104
  77.3 7.6 %copy-start.4 = (f32[32,12,720]{2,0,1:T(8,128)S(1)}, f32[32,12,720]{2,0,1:T(8,128)}, u32[]{:S(2)}) copy-start(f32[32,12,720]{2,0,1:T(8,128)} %mul.273) | copy-start | bytes 3317764
  77.3 10.6 %copy-start.1 = (f32[32,12,720]{2,0,1:T(8,128)S(1)}, f32[32,12,720]{2,0,1:T(8,128)}, u32[]{:S(2)}) copy-start(f32[32,12,720]{2,0,1:T(8,128)} %get-tuple-element.14) | copy-start | bytes 3317764
  77.3 10.6 %copy-start.2 = (f32[32,12,720]{2,0,1:T(8,128)S(1)}, f32[32,12,720]{2,0,1:T(8,128)}, u32[]{:S(2)}) copy-start(f32[32,12,720]{2,0,1:T(8,128)} %get-tuple-element.17) | copy-start | bytes 3317764
  77.3 10.6 %copy-start.3 = (f32[32,12,720]{2,0,1:T(8,128)S(1)}, f32[32,12,720]{2,0,1:T(8,128)}, u32[]{:S(2)}) copy-start(f32[32,12,720]{2,0,1:T(8,128)} %get-tuple-element.18) | copy-start | bytes 3317764
  81.3 6.6 %collective-permute-start.3 = (f32[4,1,12,720]{3,1,2,0:T(1,128)S(1)}, f32[4,1,12,720]{3,1,2,0:T(1,128)S(1)}, u32[]{:S(2)}, u32[]{:S(2)}) collective-permute-start(f32[4,1,12,720]{3,1,2,0:T(1,128)S(1)} %get-tuple-element.11), channel_id=1, source_target_pairs={{0,1},{1,2},{2,3},{3,4},{4,5},{5,6},{6,7},{7,0},{8,9},{9,10},{10,1... | collective-permute-start | bytes 414728 | tf_op jit(solution)/shard_map/ppermute | solution.py:19
  81.4 6.5 %collective-permute-start.4 = (f32[4,1,12,720]{3,1,2,0:T(1,128)S(1)}, f32[4,1,12,720]{3,1,2,0:T(1,128)S(1)}, u32[]{:S(2)}, u32[]{:S(2)}) collective-permute-start(f32[4,1,12,720]{3,1,2,0:T(1,128)S(1)} %get-tuple-element.12), channel_id=1, source_target_pairs={{1,0},{2,1},{3,2},{4,3},{5,4},{6,5},{7,6},{0,7},{9,8},{10,9},{11,1... | collective-permute-start | bytes 414728 | tf_op jit(solution)/shard_map/ppermute | solution.py:20
  107.5 7.6 %collective-permute-start.5 = (f32[4,1,12,720]{3,1,2,0:T(1,128)S(1)}, f32[4,1,12,720]{3,1,2,0:T(1,128)S(1)}, u32[]{:S(2)}, u32[]{:S(2)}) collective-permute-start(f32[4,1,12,720]{3,1,2,0:T(1,128)S(1)} %get-tuple-element.9), channel_id=1, source_target_pairs={{0,1},{1,2},{2,3},{3,4},{4,5},{5,6},{6,7},{7,0},{8,9},{9,10},{10,1... | collective-permute-start | bytes 414728 | tf_op jit(solution)/shard_map/ppermute | solution.py:19
  108.7 6.3 %collective-permute-start.6 = (f32[4,1,12,720]{3,1,2,0:T(1,128)S(1)}, f32[4,1,12,720]{3,1,2,0:T(1,128)S(1)}, u32[]{:S(2)}, u32[]{:S(2)}) collective-permute-start(f32[4,1,12,720]{3,1,2,0:T(1,128)S(1)} %get-tuple-element.10), channel_id=1, source_target_pairs={{1,0},{2,1},{3,2},{4,3},{5,4},{6,5},{7,6},{0,7},{9,8},{10,9},{11,1... | collective-permute-start | bytes 414728 | tf_op jit(solution)/shard_map/ppermute | solution.py:20
Sparse Core Ops, SparseCore 0:
  14.6 61.2 all-reduce.3
